TPU v7x, 32 devices: a whole 2x2x4 slice. The times are simulated.
32 devices in a mesh: row: 4 (over z), col: 8 (over y, x, core).
Axes of the slice: x: 2, y: 2, z: 4, core: 2. Of those that a mesh axis runs over, the one named last changes fastest.
Arguments:
- embeddings: bfloat16 [4096, 768], P(('row', 'col')), may hold values from -4 to 4
- neg_ids: int32 [4, 2048], P('row', 'col'), may hold values from 0 to 16383, as said below
- neg_counts: int32 [4], P('row'), may hold values from 256 to 2048, as said below
- index_rows: bfloat16 [16384, 768], P('row'), may hold values from -4 to 4
Outputs:
- row_loss: float32 [4096], P(('row', 'col'))
- grad: float32 [4096, 768], P(('row', 'col'))
Inputs may be any that keep to these rules, and one draw needn't show every extreme that they name: `neg_counts`: every entry lies within the range; some lists are full (2048) and some hold exactly 256 entries. Index shard of an id is id // 4096. Among the 256 slots of one device (neg_ids[b, c * 256 : (c + 1) * 256]) at most 128 ids belong to any one index shard, and in every such run exactly 128 belong to one of them.
All inputs are finite; a program needn't handle non-finite values.
Results may differ from a plain program's by a relative error of at most 0.00059.
Values may be sent and summed in bfloat16 or wider, within the bound.
A program may use at most 128 MiB of HBM per device.

v0:
```python
import jax
import jax.numpy as jnp
from jax import lax
from jax.sharding import PartitionSpec as P

D = 768


def per_device(embeddings, neg_ids, neg_counts, index_rows):
    scale = D ** (-0.5)
    n_col = lax.axis_size("col")
    shard_rows = embeddings.shape[0]
    width = embeddings.shape[1]
    row_id = lax.axis_index("row")
    col_id = lax.axis_index("col")
    queries = lax.all_gather(embeddings, "col", axis=0, tiled=True)
    keys = lax.all_gather(embeddings, "row", axis=0, tiled=True)
    query_count = queries.shape[0]
    key_count = keys.shape[0]
    requests = lax.all_gather(neg_ids, "row", axis=0, tiled=True)
    owned_count = index_rows.shape[0]
    slot_count = neg_ids.shape[1]
    local_ids = requests - row_id * owned_count
    owned = (local_ids >= 0) & (local_ids < owned_count)
    picked = jnp.take(index_rows, jnp.clip(local_ids, 0, owned_count - 1), axis=0)
    picked = jnp.where(owned[..., None], picked, jnp.zeros_like(picked))
    fetched = lax.psum_scatter(
        picked.astype(jnp.float32).astype(jnp.bfloat16), "row", scatter_dimension=0, tiled=True
    ).astype(jnp.float32)
    negatives = fetched[0].astype(jnp.bfloat16)
    row_glob = row_id * query_count + jnp.arange(query_count, dtype=jnp.int32)
    key_local = jnp.arange(key_count, dtype=jnp.int32)
    col_glob = (key_local // shard_rows * n_col + col_id) * shard_rows + key_local % shard_rows
    scores = jnp.dot(queries, keys.T, preferred_element_type=jnp.float32) * scale
    scores = jnp.where(row_glob[:, None] == col_glob[None, :], -jnp.inf, scores)
    slot_glob = col_id * slot_count + jnp.arange(slot_count, dtype=jnp.int32)
    hard = jnp.dot(queries, negatives.T, preferred_element_type=jnp.float32) * scale
    hard = jnp.where((slot_glob < neg_counts[0])[None, :], hard, -jnp.inf)
    local_top = jnp.maximum(jnp.max(scores, axis=1), jnp.max(hard, axis=1))
    top = lax.pmax(local_top, "col")
    partial_value = jnp.sum(jnp.exp(scores - top[:, None]), axis=1) + jnp.sum(
        jnp.exp(hard - top[:, None]), axis=1
    )
    total = lax.psum(partial_value, "col")
    lse = top + jnp.log(total)
    own_f = embeddings.astype(jnp.float32)
    partner = own_f.reshape(shard_rows // 2, 2, width)[:, ::-1].reshape(shard_rows, width)
    positive = jnp.sum(own_f * partner, axis=1) * scale
    own_lse = lax.dynamic_slice_in_dim(lse, col_id * shard_rows, shard_rows, 0)
    row_loss = own_lse - positive
    target = (jnp.bitwise_xor(row_glob, 1)[:, None] == col_glob[None, :]).astype(jnp.float32)
    probs_grad = (jnp.exp(scores - lse[:, None]) - target).astype(jnp.bfloat16)
    hard_probs = jnp.exp(hard - lse[:, None]).astype(jnp.bfloat16)
    term = jnp.dot(probs_grad, keys, preferred_element_type=jnp.float32)
    query_part = lax.psum_scatter(
        term + jnp.dot(hard_probs, negatives, preferred_element_type=jnp.float32),
        "col",
        scatter_dimension=0,
        tiled=True,
    )
    key_part = lax.psum_scatter(
        lax.dot_general(
            probs_grad, queries, (((0,), (0,)), ((), ())), preferred_element_type=jnp.float32
        ),
        "row",
        scatter_dimension=0,
        tiled=True,
    )
    grad = query_part + key_part
    return (row_loss, grad)


def solution(mesh):
    return jax.shard_map(
        per_device,
        mesh=mesh,
        in_specs=(P(("row", "col"), None), P("row", "col"), P("row"), P("row", None)),
        out_specs=(P(("row", "col")), P(("row", "col"), None)),
        check_vma=False,
    )
```

profile of v0, /device:TPU:0, one launch (start us, length us, event | category | flops | bytes accessed | tf_op | source)
XLA Modules:
  0.0 196.2 jit_solution(175145558935563326)
XLA Ops:
  8.0 0.0 all-gather.3.cloned.1.call-start
  8.0 0.7 all-gather.3.cloned.1.call-update
  8.7 0.0 reduce-scatter.4.cloned.1.call-start
  8.8 12.8 %all-gather = s32[4,1,256]{2,1,0:T(1,128)S(1)} all-gather(s32[1,1,256]{2,1,0:T(1,128)} %bitcast.31), channel_id=1, replica_groups=mesh['row'=4,'col'=8] {'row'}, dimensions={0}, use_global_device_ids=true | all-gather | bytes 5120 | tf_op jit(solution)/shard_map/all_gather | solution.py:20
  21.7 8.1 %gather_fusion = bf16[1024,768]{1,0:T(8,128)(2,1)S(1)} fusion(bf16[4096,768]{1,0:T(8,128)(2,1)} %param.7, s32[1024]{0:T(1024)S(1)} %broadcast_clamp_fusion), kind=kCustom, calls=%fused_computation | custom fusion | bytes 3149824 | tf_op jit(solution)/shard_map/jit(_take)/gather | solution.py:25
  29.8 0.0 copy-start
  29.8 1.4 select_select_fusion
  31.2 0.0 reduce-scatter.4.cloned.1.call-update
  31.2 0.0 reduce-scatter.8.cloned.1.call-start
  32.0 0.0 copy-done
  32.0 26.3 %all_gather.10 = bf16[512,768]{1,0:T(8,128)(2,1)S(1)} all-gather(bf16[128,768]{1,0:T(8,128)(2,1)S(1)} %copy-done), channel_id=1, replica_groups=mesh['row'=4,'col'=8] {'row'}, dimensions={0}, use_global_device_ids=true | all-gather | bytes 983040 | tf_op jit(solution)/shard_map/all_gather | solution.py:17
  58.3 0.0 copy-start.1
  58.3 0.0 all-gather.3.cloned.1.call-done
  58.3 2.7 %fusion.18 = (f32[1024]{0:T(1024)S(1)}, f32[1024,512]{0,1:T(8,128)S(1)}) fusion(bf16[1024,768]{1,0:T(8,128)(2,1)} %all-gather.3.cloned.1.call-done, bf16[512,768]{1,0:T(8,128)(2,1)S(1)} %all_gather.10, s32[512]{0:T(512)S(1)} %fusion.12, s32[1024]{0:T(1024)S(1)} %iota_add_fusion), kind=kOutput, calls=%fused_computation.43 | convolution fusion | flops 807402496 | bytes 4466688 | tf_op jit(solution)/shard_map/dot_general | solution.py:34
  61.0 0.0 copy-done.1
  61.0 12.1 %reduce-scatter.4.cloned.1.call-done = bf16[1,256,768]{2,1,0:T(8,128)(2,1)} async-done(((bf16[4,256,768]{2,1,0:T(8,128)(2,1)}), bf16[1,256,768]{2,1,0:T(8,128)(2,1)}) %reduce-scatter.4.cloned.1.call-update) | async-done | bytes 393232 | tf_op jit(solution)/shard_map/reduce_scatter | solution.py:27
  73.1 2.2 %fusion.19 = (f32[1024]{0:T(1024)S(1)}, f32[256,1024]{1,0:T(8,128)S(1)}) fusion(bf16[1024,768]{1,0:T(8,128)(2,1)} %all-gather.3.cloned.1.call-done, bf16[1,256,768]{2,1,0:T(8,128)(2,1)} %reduce-scatter.4.cloned.1.call-done, pred[256]{0:T(512)(128)(4,1)S(1)} %add_compare_fusion), kind=kOutput, calls=%fused_computation.44 | convolution fusion | flops 403438592 | bytes 3019008 | tf_op jit(solution)/shard_map/dot_general | solution.py:37
  75.3 14.0 %pmax.7 = f32[1024]{0:T(1024)S(1)} all-reduce(f32[1024]{0:T(1024)S(1)} %max.9), channel_id=1, replica_groups=mesh['row'=4,'col'=8] {'col'}, use_global_device_ids=true, to_apply=%region_3.4 | all-reduce | flops 1024 | bytes 8192 | tf_op jit(solution)/shard_map/pmax | solution.py:40
  89.2 0.2 exponential_reduce_fusion.1
  89.4 0.3 exponential_reduce_fusion
  89.7 11.8 %psum.7 = f32[1024]{0:T(1024)S(1)} all-reduce(f32[1024]{0:T(1024)S(1)} %add.93), channel_id=1, replica_groups=mesh['row'=4,'col'=8] {'col'}, use_global_device_ids=true, to_apply=%region_6.7 | all-reduce | flops 1024 | bytes 8192 | tf_op jit(solution)/shard_map/psum | solution.py:44
  101.5 3.8 %fusion.16 = f32[512,768]{1,0:T(8,128)} fusion(bf16[1024,768]{1,0:T(8,128)(2,1)} %all-gather.3.cloned.1.call-done, f32[1024,512]{0,1:T(8,128)S(1)} %get-tuple-element.3, s32[1024]{0:T(1024)S(1)} %broadcast_xor_fusion, f32[1024]{0:T(1024)S(1)} %log_add_fusion, s32[512]{0:T(512)S(1)} %fusion.12), kind=kOutput, calls=%fused_computation.41 | convolution fusion | flops 807927808 | bytes 5253120 | tf_op jit(solution)/shard_map/dot_general | solution.py:62
  105.3 0.0 reduce-scatter.8.cloned.1.call-update
  105.3 0.0 reduce-scatter.6.cloned.1.call-start
  105.4 0.0 copy-start.2
  105.4 2.3 %fusion.17 = f32[1024,768]{1,0:T(8,128)S(1)} fusion(bf16[512,768]{1,0:T(8,128)(2,1)} %copy-done.1, f32[1024,512]{0,1:T(8,128)S(1)} %get-tuple-element.3, s32[1024]{0:T(1024)S(1)} %broadcast_xor_fusion, f32[1024]{0:T(1024)S(1)} %log_add_fusion, s32[512]{0:T(512)S(1)} %fusion.12), kind=kOutput, calls=%fused_computation.42 | convolution fusion | flops 807927808 | bytes 6039552 | tf_op jit(solution)/shard_map/dot_general | solution.py:54
  107.7 0.0 copy-done.2
  107.7 2.3 %convolution_add_fusion = f32[1024,768]{1,0:T(8,128)} fusion(f32[1024,768]{1,0:T(8,128)S(1)} %fusion.17, f32[256,1024]{1,0:T(8,128)S(1)} %get-tuple-element.5, f32[1024]{0:T(1024)S(1)} %log_add_fusion, bf16[1,256,768]{2,1,0:T(8,128)(2,1)S(1)} %copy-done.2), kind=kOutput, calls=%fused_computation.4 | convolution fusion | flops 403963904 | bytes 7737344 | tf_op jit(solution)/shard_map/dot_general | solution.py:56
  110.0 0.0 reduce-scatter.6.cloned.1.call-update
  110.0 0.2 reshape.55
  110.2 1.1 rev.3
  111.4 0.3 reshape.56
  111.6 0.1 multiply_reduce_fusion
  111.8 0.6 multiply_subtract_fusion
  112.3 26.1 %reduce-scatter.8.cloned.1.call-done = f32[128,768]{1,0:T(8,128)} async-done(((f32[512,768]{1,0:T(8,128)}), f32[128,768]{1,0:T(8,128)}) %reduce-scatter.8.cloned.1.call-update) | async-done | bytes 393232 | tf_op jit(solution)/shard_map/reduce_scatter | solution.py:61
  138.4 48.2 %reduce-scatter.6.cloned.1.call-done = f32[128,768]{1,0:T(8,128)} async-done(((f32[1024,768]{1,0:T(8,128)}), f32[128,768]{1,0:T(8,128)}) %reduce-scatter.6.cloned.1.call-update) | async-done | bytes 393232 | tf_op jit(solution)/shard_map/reduce_scatter | solution.py:55
  186.7 1.9 add.97
  (14 shorter events, 0.1 us)
Async XLA Ops:
  8.0 50.3 %all-gather.3.cloned.1.call-start = ((), (), s32[]{:S(2)}) async-start(), calls=%async_computation.3 | async-start | bytes 1769472 | tf_op jit(solution)/shard_map/all_gather | solution.py:16
  8.7 64.4 %reduce-scatter.4.cloned.1.call-start = ((), (), s32[]{:S(2)}) async-start(), calls=%async_computation.4 | async-start | bytes 1966080 | tf_op jit(solution)/shard_map/reduce_scatter | solution.py:27
  29.8 2.2 %copy-start = (bf16[128,768]{1,0:T(8,128)(2,1)S(1)}, bf16[128,768]{1,0:T(8,128)(2,1)}, u32[]{:S(2)}) copy-start(bf16[128,768]{1,0:T(8,128)(2,1)} %param.4) | copy-start | bytes 589828
  31.2 107.2 %reduce-scatter.8.cloned.1.call-start = ((), (), s32[]{:S(2)}) async-start(), calls=%async_computation.6 | async-start | bytes 1966080 | tf_op jit(solution)/shard_map/reduce_scatter | solution.py:61
  58.3 2.7 %copy-start.1 = (bf16[512,768]{1,0:T(8,128)(2,1)}, bf16[512,768]{1,0:T(8,128)(2,1)S(1)}, u32[]{:S(2)}) copy-start(bf16[512,768]{1,0:T(8,128)(2,1)S(1)} %all_gather.10) | copy-start | bytes 2359300
  105.3 81.4 %reduce-scatter.6.cloned.1.call-start = ((), (), s32[]{:S(2)}) async-start(), calls=%async_computation.5 | async-start | bytes 3538944 | tf_op jit(solution)/shard_map/reduce_scatter | solution.py:55
  105.4 2.3 %copy-start.2 = (bf16[1,256,768]{2,1,0:T(8,128)(2,1)S(1)}, bf16[1,256,768]{2,1,0:T(8,128)(2,1)}, u32[]{:S(2)}) copy-start(bf16[1,256,768]{2,1,0:T(8,128)(2,1)} %reduce-scatter.4.cloned.1.call-done) | copy-start | bytes 1179652
Sparse Core Ops, SparseCore 0:
  10.7 28.4 all-gather.2
Sparse Core Ops, SparseCore 1:
  31.3 41.7 reduce-scatter.3
  105.4 33.0 reduce-scatter.7
  141.7 44.9 reduce-scatter.5
where the time goes:
time: 197 us; the launch traced here: 196 us
  waiting for transfers between devices  87.1 us (44%)
  blocking collectives  64.9 us (33%)
  between operations  16.5 us (8%)
  matrix products  13.3 us (7%)
  local copies, waits for them, and re-layouts  9.65 us (5%)
  other arithmetic  4.59 us (2%)
    reduce_scatter x1, waiting for transfers between devices, per_device(): lax.psum_scatter(term + jnp.dot(hard_probs, negatives, preferred_element_...  48.2 us
    all_gather x1, blocking collectives, per_device(): keys = lax.all_gather(embeddings, 'row', axis=0, tiled=True)  26.3 us
    reduce_scatter x1, waiting for transfers between devices, per_device(): lax.psum_scatter(lax.dot_general(probs_grad, queries, (((0,), (0,)), ((),...  26.1 us
    pmax x1, blocking collectives, per_device(): top = lax.pmax(local_top, 'col')  14 us
    all_gather x1, blocking collectives, per_device(): requests = lax.all_gather(neg_ids, 'row', axis=0, tiled=True)  12.8 us
    reduce_scatter x1, waiting for transfers between devices, per_device(): lax.psum_scatter(picked.astype(jnp.float32).astype(jnp.bfloat16), 'row',...  12.1 us
    psum x1, blocking collectives, per_device(): total = lax.psum(partial_value, 'col')  11.8 us
    gather x1, local copies, waits for them, and re-layouts, per_device(): jnp.take(index_rows, jnp.clip(local_ids, 0, owned_count - 1), axis=0)  8.07 us
  transfers between devices with their start and end apart: 4, of which 3 were waited for; matrix products, arithmetic and copies ran while one was open for 10% of the time, Pallas kernels for 0%

commit v1 on v0

--- a/solution.py
+++ b/solution.py
@@ -4,6 +4,16 @@
 from jax.sharding import PartitionSpec as P
 
 D = 768
+
+
+def manage_values_all(inner_x):
+    dev_axis = "col"
+    world_n = lax.psum(1, dev_axis)
+    before = lambda w2: [(src_i, src_i ^ w2) for src_i in range(world_n)]
+    long_array = inner_x
+    for pp in range(world_n.bit_length() - 1):
+        long_array = long_array + lax.ppermute(long_array, dev_axis, before(1 << pp))
+    return long_array
 
 
 def per_device(embeddings, neg_ids, neg_counts, index_rows):
@@ -41,7 +51,7 @@
     partial_value = jnp.sum(jnp.exp(scores - top[:, None]), axis=1) + jnp.sum(
         jnp.exp(hard - top[:, None]), axis=1
     )
-    total = lax.psum(partial_value, "col")
+    total = manage_values_all(partial_value)
     lse = top + jnp.log(total)
     own_f = embeddings.astype(jnp.float32)
     partner = own_f.reshape(shard_rows // 2, 2, width)[:, ::-1].reshape(shard_rows, width)

time: 197 us -> 192 us (0.975)
  blocking collectives: 64.9 us -> 53.1 us
  waiting for transfers between devices: 87.1 us -> 95 us
    psum x1 -> x0, blocking collectives: 11.8 us -> none  [per_device(): total = lax.psum(partial_value, 'col')]
    ppermute x0 -> x3, waiting for transfers between devices: none -> 7.88 us  [manage_values_all(): lax.ppermute(long_array, dev_axis, before(1 << pp))]
  transfers between devices with their start and end apart: 4 -> 7, of which waited for: 3 -> 6; matrix products, arithmetic and copies ran while one was open for 10% -> 10% of each run, Pallas kernels for 0% -> 0%
where the time goes in v1:
time: 192 us; the launch traced here: 191 us
  waiting for transfers between devices  95 us (49%)
  blocking collectives  53.1 us (28%)
  between operations  16.5 us (9%)
  matrix products  11.9 us (6%)
  local copies, waits for them, and re-layouts  9.66 us (5%)
  other arithmetic  4.57 us (2%)
    reduce_scatter x1, waiting for transfers between devices, per_device(): lax.psum_scatter(term + jnp.dot(hard_probs, negatives, preferred_element_...  48.2 us
    all_gather x1, blocking collectives, per_device(): keys = lax.all_gather(embeddings, 'row', axis=0, tiled=True)  26.3 us
    reduce_scatter x1, waiting for transfers between devices, per_device(): lax.psum_scatter(lax.dot_general(probs_grad, queries, (((0,), (0,)), ((),...  26.1 us
    pmax x1, blocking collectives, per_device(): top = lax.pmax(local_top, 'col')  14 us
    all_gather x1, blocking collectives, per_device(): requests = lax.all_gather(neg_ids, 'row', axis=0, tiled=True)  12.8 us
    reduce_scatter x1, waiting for transfers between devices, per_device(): lax.psum_scatter(picked.astype(jnp.float32).astype(jnp.bfloat16), 'row',...  12.1 us
    gather x1, local copies, waits for them, and re-layouts, per_device(): jnp.take(index_rows, jnp.clip(local_ids, 0, owned_count - 1), axis=0)  8.07 us
    ppermute x3, waiting for transfers between devices, manage_values_all(): lax.ppermute(long_array, dev_axis, before(1 << pp))  7.88 us
  transfers between devices with their start and end apart: 7, of which 6 were waited for; matrix products, arithmetic and copies ran while one was open for 10% of the time, Pallas kernels for 0%

profile of v1, /device:TPU:0, one launch (start us, length us, event | category | flops | bytes accessed | tf_op | source)
XLA Modules:
  0.0 191.4 jit_solution(9554369878068623590)
XLA Ops:
  8.0 0.0 all-gather.3.cloned.1.call-start
  8.0 0.7 all-gather.3.cloned.1.call-update
  8.7 0.0 reduce-scatter.4.cloned.1.call-start
  8.8 12.8 %all-gather = s32[4,1,256]{2,1,0:T(1,128)S(1)} all-gather(s32[1,1,256]{2,1,0:T(1,128)} %bitcast.31), channel_id=1, replica_groups=mesh['row'=4,'col'=8] {'row'}, dimensions={0}, use_global_device_ids=true | all-gather | bytes 5120 | tf_op jit(solution)/shard_map/all_gather | solution.py:30
  21.7 8.1 %gather_fusion = bf16[1024,768]{1,0:T(8,128)(2,1)S(1)} fusion(bf16[4096,768]{1,0:T(8,128)(2,1)} %param.7, s32[1024]{0:T(1024)S(1)} %broadcast_clamp_fusion), kind=kCustom, calls=%fused_computation | custom fusion | bytes 3149824 | tf_op jit(solution)/shard_map/jit(_take)/gather | solution.py:35
  29.8 0.0 copy-start
  29.8 1.4 select_select_fusion
  31.2 0.0 reduce-scatter.4.cloned.1.call-update
  31.2 0.0 reduce-scatter.8.cloned.1.call-start
  32.0 0.0 copy-done
  32.0 26.3 %all_gather.10 = bf16[512,768]{1,0:T(8,128)(2,1)S(1)} all-gather(bf16[128,768]{1,0:T(8,128)(2,1)S(1)} %copy-done), channel_id=1, replica_groups=mesh['row'=4,'col'=8] {'row'}, dimensions={0}, use_global_device_ids=true | all-gather | bytes 983040 | tf_op jit(solution)/shard_map/all_gather | solution.py:27
  58.2 0.0 copy-start.1
  58.2 0.0 all-gather.3.cloned.1.call-done
  58.2 2.7 %fusion.18 = (f32[1024]{0:T(1024)S(1)}, f32[1024,512]{0,1:T(8,128)S(1)}) fusion(bf16[1024,768]{1,0:T(8,128)(2,1)} %all-gather.3.cloned.1.call-done, bf16[512,768]{1,0:T(8,128)(2,1)S(1)} %all_gather.10, s32[512]{0:T(512)S(1)} %fusion.12, s32[1024]{0:T(1024)S(1)} %iota_add_fusion), kind=kOutput, calls=%fused_computation.43 | convolution fusion | flops 807402496 | bytes 4466688 | tf_op jit(solution)/shard_map/dot_general | solution.py:44
  61.0 0.0 copy-done.1
  61.0 12.1 %reduce-scatter.4.cloned.1.call-done = bf16[1,256,768]{2,1,0:T(8,128)(2,1)} async-done(((bf16[4,256,768]{2,1,0:T(8,128)(2,1)}), bf16[1,256,768]{2,1,0:T(8,128)(2,1)}) %reduce-scatter.4.cloned.1.call-update) | async-done | bytes 393232 | tf_op jit(solution)/shard_map/reduce_scatter | solution.py:37
  73.0 2.2 %fusion.19 = (f32[1024]{0:T(1024)S(1)}, f32[256,1024]{1,0:T(8,128)S(1)}) fusion(bf16[1024,768]{1,0:T(8,128)(2,1)} %all-gather.3.cloned.1.call-done, bf16[1,256,768]{2,1,0:T(8,128)(2,1)} %reduce-scatter.4.cloned.1.call-done, pred[256]{0:T(512)(128)(4,1)S(1)} %add_compare_fusion), kind=kOutput, calls=%fused_computation.44 | convolution fusion | flops 403438592 | bytes 3019008 | tf_op jit(solution)/shard_map/dot_general | solution.py:47
  75.2 14.0 %pmax.7 = f32[1024]{0:T(1024)S(1)} all-reduce(f32[1024]{0:T(1024)S(1)} %max.9), channel_id=1, replica_groups=mesh['row'=4,'col'=8] {'col'}, use_global_device_ids=true, to_apply=%region_3.4 | all-reduce | flops 1024 | bytes 8192 | tf_op jit(solution)/shard_map/pmax | solution.py:50
  89.2 0.0 copy-start.3
  89.2 0.2 exponential_reduce_fusion.1
  89.4 0.3 exponential_reduce_fusion
  89.7 0.1 collective-permute-start
  89.8 1.2 collective-permute-done
  90.9 0.0 collective-permute-start.1
  90.9 3.6 %collective-permute-done.1 = f32[1024]{0:T(1024)S(1)} collective-permute-done((f32[1024]{0:T(1024)S(1)}, f32[1024]{0:T(1024)S(1)}, u32[]{:S(2)}, u32[]{:S(2)}) %collective-permute-start.1) | collective-permute-done | bytes 4128 | tf_op jit(solution)/shard_map/ppermute | solution.py:15
  94.5 0.5 collective-permute-start.2
  95.0 3.1 %collective-permute-done.2 = f32[1024]{0:T(1024)S(1)} collective-permute-done((f32[1024]{0:T(1024)S(1)}, f32[1024]{0:T(1024)S(1)}, u32[]{:S(2)}, u32[]{:S(2)}) %collective-permute-start.2) | collective-permute-done | bytes 4128 | tf_op jit(solution)/shard_map/ppermute | solution.py:15
  98.2 0.0 copy-done.3
  98.2 2.4 %fusion.16 = f32[512,768]{1,0:T(8,128)} fusion(bf16[1024,768]{1,0:T(8,128)(2,1)S(1)} %copy-done.3, f32[1024,512]{0,1:T(8,128)S(1)} %get-tuple-element.3, s32[1024]{0:T(1024)S(1)} %broadcast_xor_fusion, f32[1024]{0:T(1024)S(1)} %log_add_fusion, s32[512]{0:T(512)S(1)} %fusion.12), kind=kOutput, calls=%fused_computation.41 | convolution fusion | flops 807927808 | bytes 5253120 | tf_op jit(solution)/shard_map/dot_general | solution.py:72
  100.6 0.0 reduce-scatter.8.cloned.1.call-update
  100.6 0.0 reduce-scatter.6.cloned.1.call-start
  100.6 0.0 copy-start.2
  100.6 2.3 %fusion.17 = f32[1024,768]{1,0:T(8,128)S(1)} fusion(bf16[512,768]{1,0:T(8,128)(2,1)} %copy-done.1, f32[1024,512]{0,1:T(8,128)S(1)} %get-tuple-element.3, s32[1024]{0:T(1024)S(1)} %broadcast_xor_fusion, f32[1024]{0:T(1024)S(1)} %log_add_fusion, s32[512]{0:T(512)S(1)} %fusion.12), kind=kOutput, calls=%fused_computation.42 | convolution fusion | flops 807927808 | bytes 6039552 | tf_op jit(solution)/shard_map/dot_general | solution.py:64
  102.9 0.0 copy-done.2
  103.0 2.3 %convolution_add_fusion = f32[1024,768]{1,0:T(8,128)} fusion(f32[1024,768]{1,0:T(8,128)S(1)} %fusion.17, f32[256,1024]{1,0:T(8,128)S(1)} %get-tuple-element.5, f32[1024]{0:T(1024)S(1)} %log_add_fusion, bf16[1,256,768]{2,1,0:T(8,128)(2,1)S(1)} %copy-done.2), kind=kOutput, calls=%fused_computation.4 | convolution fusion | flops 403963904 | bytes 7737344 | tf_op jit(solution)/shard_map/dot_general | solution.py:66
  105.3 0.0 reduce-scatter.6.cloned.1.call-update
  105.3 0.2 reshape.55
  105.5 1.1 rev.3
  106.6 0.3 reshape.56
  106.9 0.1 multiply_reduce_fusion
  107.0 0.6 multiply_subtract_fusion
  107.6 26.1 %reduce-scatter.8.cloned.1.call-done = f32[128,768]{1,0:T(8,128)} async-done(((f32[512,768]{1,0:T(8,128)}), f32[128,768]{1,0:T(8,128)}) %reduce-scatter.8.cloned.1.call-update) | async-done | bytes 393232 | tf_op jit(solution)/shard_map/reduce_scatter | solution.py:71
  133.7 48.2 %reduce-scatter.6.cloned.1.call-done = f32[128,768]{1,0:T(8,128)} async-done(((f32[1024,768]{1,0:T(8,128)}), f32[128,768]{1,0:T(8,128)}) %reduce-scatter.6.cloned.1.call-update) | async-done | bytes 393232 | tf_op jit(solution)/shard_map/reduce_scatter | solution.py:65
  181.9 1.9 add.107
  (16 shorter events, 0.1 us)
Async XLA Ops:
  8.0 50.2 %all-gather.3.cloned.1.call-start = ((), (), s32[]{:S(2)}) async-start(), calls=%async_computation.3 | async-start | bytes 1769472 | tf_op jit(solution)/shard_map/all_gather | solution.py:26
  8.7 64.3 %reduce-scatter.4.cloned.1.call-start = ((), (), s32[]{:S(2)}) async-start(), calls=%async_computation.4 | async-start | bytes 1966080 | tf_op jit(solution)/shard_map/reduce_scatter | solution.py:37
  29.8 2.1 %copy-start = (bf16[128,768]{1,0:T(8,128)(2,1)S(1)}, bf16[128,768]{1,0:T(8,128)(2,1)}, u32[]{:S(2)}) copy-start(bf16[128,768]{1,0:T(8,128)(2,1)} %param.4) | copy-start | bytes 589828
  31.2 102.5 %reduce-scatter.8.cloned.1.call-start = ((), (), s32[]{:S(2)}) async-start(), calls=%async_computation.6 | async-start | bytes 1966080 | tf_op jit(solution)/shard_map/reduce_scatter | solution.py:71
  58.2 2.7 %copy-start.1 = (bf16[512,768]{1,0:T(8,128)(2,1)}, bf16[512,768]{1,0:T(8,128)(2,1)S(1)}, u32[]{:S(2)}) copy-start(bf16[512,768]{1,0:T(8,128)(2,1)S(1)} %all_gather.10) | copy-start | bytes 2359300
  89.2 9.0 %copy-start.3 = (bf16[1024,768]{1,0:T(8,128)(2,1)S(1)}, bf16[1024,768]{1,0:T(8,128)(2,1)}, u32[]{:S(2)}) copy-start(bf16[1024,768]{1,0:T(8,128)(2,1)} %all-gather.3.cloned.1.call-done) | copy-start | bytes 4718596
  89.7 1.2 collective-permute-start
  90.9 3.6 %collective-permute-start.1 = (f32[1024]{0:T(1024)S(1)}, f32[1024]{0:T(1024)S(1)}, u32[]{:S(2)}, u32[]{:S(2)}) collective-permute-start(f32[1024]{0:T(1024)S(1)} %add.101), channel_id=1, source_target_pairs={{0,2},{1,3},{2,0},{3,1},{4,6},{5,7},{6,4},{7,5},{8,10},{9,11},{10,... | collective-permute-start | bytes 12296 | tf_op jit(solution)/shard_map/ppermute | solution.py:15
  94.5 3.6 %collective-permute-start.2 = (f32[1024]{0:T(1024)S(1)}, f32[1024]{0:T(1024)S(1)}, u32[]{:S(2)}, u32[]{:S(2)}) collective-permute-start(f32[1024]{0:T(1024)S(1)} %add.102), channel_id=1, source_target_pairs={{0,4},{1,5},{2,6},{3,7},{4,0},{5,1},{6,2},{7,3},{8,12},{9,13},{10,... | collective-permute-start | bytes 12296 | tf_op jit(solution)/shard_map/ppermute | solution.py:15
  100.6 81.4 %reduce-scatter.6.cloned.1.call-start = ((), (), s32[]{:S(2)}) async-start(), calls=%async_computation.5 | async-start | bytes 3538944 | tf_op jit(solution)/shard_map/reduce_scatter | solution.py:65
  100.6 2.3 %copy-start.2 = (bf16[1,256,768]{2,1,0:T(8,128)(2,1)S(1)}, bf16[1,256,768]{2,1,0:T(8,128)(2,1)}, u32[]{:S(2)}) copy-start(bf16[1,256,768]{2,1,0:T(8,128)(2,1)} %reduce-scatter.4.cloned.1.call-done) | copy-start | bytes 1179652
Sparse Core Ops, SparseCore 0:
  10.7 28.4 all-gather.2
Sparse Core Ops, SparseCore 1:
  31.3 41.7 reduce-scatter.3
  100.7 33.0 reduce-scatter.7
  137.0 44.9 reduce-scatter.5
